TPU v7x, 32 devices: a whole 2x2x4 slice. The times are simulated.
32 devices in a mesh: dp: 4 (over z), cell: 8 (over y, x, core).
Axes of the slice: x: 2, y: 2, z: 4, core: 2. Of those that a mesh axis runs over, the one named last changes fastest.
Arguments:
- sensitivity: float32 [1024, 65536], P(('dp', 'cell')), may hold values from -0.046875 to 0.046875
- row_period: int32 [1024], P(('dp', 'cell')), may hold values from 0 to 31
- row_site: int32 [1024], P(('dp', 'cell')), may hold values from 0 to 127
- period_err: float32 [32], replicated, may hold values from 0.2 to 2
- site_err: float32 [128], replicated, may hold values from 0.2 to 2
- cell_var: float32 [65536], replicated, may hold values from 0.25 to 4
- cell_perm: int32 [65536], replicated, may hold values from 0 to 65535, each once
Outputs:
- gram: float32 [1024, 1024], P('cell', 'dp')
Inputs may be any that keep to these rules, and one draw needn't show every extreme that they name: `cell_perm`: a permutation of 0 to 65535.
All inputs are finite; a program needn't handle non-finite values.
Results may differ from a plain program's by a relative error of at most 0.0009.
Values may be sent and summed in bfloat16 or wider, within the bound.
A program may use at most 128 MiB of HBM per device.

v0:
```python
import jax
import jax.numpy as jnp
from jax import lax
from jax.sharding import PartitionSpec as P


def pack_rows(sensitivity, row_period, row_site, period_err, site_err):
    period_hit = row_period[:, None] == jnp.arange(period_err.shape[0], dtype=jnp.int32)[None, :]
    site_hit = row_site[:, None] == jnp.arange(site_err.shape[0], dtype=jnp.int32)[None, :]
    period_scale = jnp.sum(jnp.where(period_hit, period_err[None, :], 0.0), axis=1)
    site_scale = jnp.sum(jnp.where(site_hit, site_err[None, :], 0.0), axis=1)
    row_weight = 1.0 / jnp.sqrt(period_scale * period_scale + site_scale * site_scale)
    return (row_weight[:, None] * sensitivity).astype(jnp.bfloat16)


def weigh_columns(scaled, cell_var, cell_perm, first_cell):
    width = scaled.shape[1]
    positions = lax.dynamic_slice_in_dim(cell_perm, first_cell, width)
    column_var = cell_var[positions]
    return (scaled.astype(jnp.float32) * column_var[None, :]).astype(jnp.bfloat16)


def against(rows_block, weighted):
    return lax.dot_general(
        rows_block, weighted, (((1,), (1,)), ((), ())), preferred_element_type=jnp.float32
    )


def body(sensitivity, row_period, row_site, period_err, site_err, cell_var, cell_perm):
    packed = pack_rows(sensitivity, row_period, row_site, period_err, site_err)
    total_cells = cell_var.shape[0]
    scaled = lax.all_to_all(packed, "cell", split_axis=1, concat_axis=0, tiled=True)
    first_cell = lax.axis_index("cell") * (total_cells // lax.axis_size("cell"))
    weighted = weigh_columns(scaled, cell_var, cell_perm, first_cell)
    partial_value = against(lax.all_gather(scaled, "dp", axis=0, tiled=True), weighted)
    gram = lax.psum_scatter(partial_value, "cell", scatter_dimension=0, tiled=True)
    return gram


def solution(mesh):
    return jax.shard_map(
        body,
        mesh=mesh,
        in_specs=(
            P(("dp", "cell"), None),
            P(("dp", "cell")),
            P(("dp", "cell")),
            P(),
            P(),
            P(),
            P(),
        ),
        out_specs=P("cell", "dp"),
        check_vma=False,
    )
```

profile of v0, /device:TPU:0, one launch (start us, length us, event | category | flops | bytes accessed | tf_op | source)
XLA Modules:
  0.0 406.7 jit_solution(11270478150650060878)
XLA Ops:
  6.5 0.0 copy-start
  6.5 0.0 all-gather.2.cloned.1.call-start
  6.5 0.9 select_reduce_fusion.1
  7.4 0.9 select_reduce_fusion
  8.3 3.9 multiply_convert_fusion.1
  12.2 0.3 copy.13
  12.5 54.1 %all_to_all.19 = bf16[32,8,8192]{2,0,1:T(8,128)(2,1)} all-to-all(bf16[32,8,8192]{2,0,1:T(8,128)(2,1)S(1)} %bitcast.11), channel_id=1, replica_groups=mesh['dp'=4,'cell'=8] {'cell'}, dimensions={1} | all-to-all | bytes 8388608 | tf_op jit(solution)/shard_map/all_to_all | solution.py:32
  66.7 0.0 all-gather.2.cloned.1.call-update
  66.7 0.0 reduce-scatter.2.cloned.1.call-start
  66.7 0.8 fusion.2
  67.5 0.0 copy-done
  67.5 45.5 %gather_fusion = f32[8192]{0:T(1024)S(1)} fusion(f32[65536]{0:T(1024)S(1)} %copy-done, s32[8192]{0:T(1024)S(1)} %fusion.2), kind=kCustom, calls=%fused_computation | custom fusion | bytes 98304 | tf_op jit(solution)/shard_map/gather | solution.py:19
  113.1 239.9 %all-gather.2.cloned.1.call-done = bf16[1024,8192]{1,0:T(8,128)(2,1)} async-done(((bf16[256,8192]{1,0:T(8,128)(2,1)}), bf16[1024,8192]{1,0:T(8,128)(2,1)}) %all-gather.2.cloned.1.call-update) | async-done | bytes 16777232 | tf_op jit(solution)/shard_map/all_gather | solution.py:35
  353.0 12.5 %fusion = f32[1024,256]{1,0:T(8,128)} fusion(bf16[1024,8192]{1,0:T(8,128)(2,1)} %all-gather.2.cloned.1.call-done, bf16[256,8192]{1,0:T(8,128)(2,1)} %bitcast.9, f32[8192]{0:T(1024)S(1)} %gather_fusion), kind=kOutput, calls=%fused_computation.3 | convolution fusion | flops 4301258752 | bytes 22052864 | tf_op jit(solution)/shard_map/dot_general | solution.py:24
  365.4 0.0 reduce-scatter.2.cloned.1.call-update
  365.5 34.4 %reduce-scatter.2.cloned.1.call-done = f32[128,256]{1,0:T(8,128)} async-done(((f32[1024,256]{1,0:T(8,128)}), f32[128,256]{1,0:T(8,128)}) %reduce-scatter.2.cloned.1.call-update) | async-done | bytes 131088 | tf_op jit(solution)/shard_map/reduce_scatter | solution.py:36
  (1 shorter events, 0.0 us)
Async XLA Ops:
  6.5 61.0 %copy-start = (f32[65536]{0:T(1024)S(1)}, f32[65536]{0:T(1024)}, u32[]{:S(2)}) copy-start(f32[65536]{0:T(1024)} %param.12) | copy-start | bytes 786436
  6.5 346.4 %all-gather.2.cloned.1.call-start = ((), (), s32[]{:S(2)}) async-start(), calls=%async_computation.2 | async-start | bytes 20971520 | tf_op jit(solution)/shard_map/all_gather | solution.py:35
  66.7 333.2 %reduce-scatter.2.cloned.1.call-start = ((), (), s32[]{:S(2)}) async-start(), calls=%async_computation.3 | async-start | bytes 1179648 | tf_op jit(solution)/shard_map/reduce_scatter | solution.py:36
Sparse Core Ops, SparseCore 0:
  66.8 286.1 all-gather.1
  365.6 34.2 reduce-scatter.1
where the time goes:
time: 407 us
  waiting for transfers between devices  274 us (67%)
  blocking collectives  54.1 us (13%)
  local copies, waits for them, and re-layouts  45.8 us (11%)
  between operations  13.4 us (3%)
  matrix products  12.5 us (3%)
  other arithmetic  6.46 us (2%)
    all_gather x1, waiting for transfers between devices, body(): lax.all_gather(scaled, 'dp', axis=0, tiled=True)  240 us
    all_to_all x1, blocking collectives, body(): lax.all_to_all(packed, 'cell', split_axis=1, concat_axis=0, tiled=True)  54.1 us
    gather x1, local copies, waits for them, and re-layouts, weigh_columns(): column_var = cell_var[positions]  45.5 us
    reduce_scatter x1, waiting for transfers between devices, body(): lax.psum_scatter(partial_value, 'cell', scatter_dimension=0, tiled=True)  34.4 us
    dot_general x1, matrix products, against(): lax.dot_general(rows_block, weighted, (((1,), (1,)), ((), ())), preferred...  12.5 us
  transfers between devices with their start and end apart: 2, of which 2 were waited for; matrix products, arithmetic and copies ran while one was open for 11% of the time, Pallas kernels for 0%

commit v1 on v0

--- a/solution.py
+++ b/solution.py
@@ -1,15 +1,25 @@
+import functools
 import jax
 import jax.numpy as jnp
 from jax import lax
+from jax.experimental import pallas as pl
+from jax.experimental.pallas import tpu as pltpu
 from jax.sharding import PartitionSpec as P
 
-
-def pack_rows(sensitivity, row_period, row_site, period_err, site_err):
+MESH = pl.DeviceIdType.MESH
+VMEM_BUDGET = 56 * 1024 * 1024
+
+
+def weigh_rows(row_period, row_site, period_err, site_err):
     period_hit = row_period[:, None] == jnp.arange(period_err.shape[0], dtype=jnp.int32)[None, :]
     site_hit = row_site[:, None] == jnp.arange(site_err.shape[0], dtype=jnp.int32)[None, :]
     period_scale = jnp.sum(jnp.where(period_hit, period_err[None, :], 0.0), axis=1)
     site_scale = jnp.sum(jnp.where(site_hit, site_err[None, :], 0.0), axis=1)
-    row_weight = 1.0 / jnp.sqrt(period_scale * period_scale + site_scale * site_scale)
+    return 1.0 / jnp.sqrt(period_scale * period_scale + site_scale * site_scale)
+
+
+def pack_rows(sensitivity, row_period, row_site, period_err, site_err):
+    row_weight = weigh_rows(row_period, row_site, period_err, site_err)
     return (row_weight[:, None] * sensitivity).astype(jnp.bfloat16)
 
 
@@ -26,7 +36,7 @@
     )
 
 
-def body(sensitivity, row_period, row_site, period_err, site_err, cell_var, cell_perm):
+def body_general(sensitivity, row_period, row_site, period_err, site_err, cell_var, cell_perm):
     packed = pack_rows(sensitivity, row_period, row_site, period_err, site_err)
     total_cells = cell_var.shape[0]
     scaled = lax.all_to_all(packed, "cell", split_axis=1, concat_axis=0, tiled=True)
@@ -35,6 +45,259 @@
     partial_value = against(lax.all_gather(scaled, "dp", axis=0, tiled=True), weighted)
     gram = lax.psum_scatter(partial_value, "cell", scatter_dimension=0, tiled=True)
     return gram
+
+
+def flip(index, mask):
+    bit = 1
+    while bit <= mask:
+        if mask & bit:
+            index = index + (1 - 2 * ((index // bit) % 2)) * bit
+        bit *= 2
+    return index
+
+
+def subsets(bits):
+    masks = [0]
+    for bit in bits:
+        masks = masks + [mask | (1 << bit) for mask in masks]
+    return masks
+
+
+def halvings(n_cell):
+    levels = n_cell.bit_length() - 1
+    rest = list(range(1, levels))
+    orders = (rest, rest[::-1])
+    rounds = [[(0, rest, None)]]
+    for depth in range(len(rest)):
+        rounds.append([(order[depth], order[depth + 1:], half) for half, order in enumerate(orders)])
+    return rounds
+
+
+def gram_kernel(
+    n_dp, n_cell,
+    sens_ref, weight_ref, perm_ref, table_ref, out_ref,
+    stage, outgoing, rows, weighted, column_var, partial, *rest,
+):
+    rounds = halvings(n_cell)
+    n_bufs = sum(len(steps) for steps in rounds)
+    bufs, (z_buf, load_sem, send_sem, recv_sem, rs_send, rs_recv, z_send, z_recv) = rest[:n_bufs], rest[n_bufs:]
+    dp, cell = lax.axis_index("dp"), lax.axis_index("cell")
+    n_rows, n_all = sens_ref.shape
+    width = n_all // (n_dp * n_cell)
+    plane = n_cell * n_rows
+    n_total = n_dp * plane
+    send_order = sorted(range(n_dp), key=lambda m: (m == 0, -m))
+
+    barrier = pltpu.get_barrier_semaphore()
+    for m in range(n_dp):
+        for c in range(n_cell):
+            if m or c:
+                pl.semaphore_signal(barrier, inc=1, device_id=(flip(dp, m), flip(cell, c)), device_id_type=MESH)
+
+    def load(m):
+        first = pl.multiple_of(flip(dp, m) * (n_cell * width), 128)
+        return pltpu.make_async_copy(sens_ref.at[:, pl.ds(first, n_cell * width)], stage.at[m], load_sem.at[m])
+
+    for m in send_order:
+        load(m).start()
+
+    def transfer(m, c):
+        return pltpu.make_async_remote_copy(
+            src_ref=outgoing.at[m, c],
+            dst_ref=rows.at[dp * n_cell + cell],
+            send_sem=send_sem.at[m, c],
+            recv_sem=recv_sem.at[m, c],
+            device_id=(flip(dp, m), flip(cell, c)),
+            device_id_type=MESH,
+        )
+
+    def arrival(m, c):
+        return pltpu.make_async_remote_copy(
+            src_ref=outgoing.at[m, c],
+            dst_ref=rows.at[flip(dp, m) * n_cell + flip(cell, c)],
+            send_sem=send_sem.at[m, c],
+            recv_sem=recv_sem.at[m, c],
+            device_id=(flip(dp, m), flip(cell, c)),
+            device_id_type=MESH,
+        )
+
+    weight = weight_ref[...]
+    for place, m in enumerate(send_order):
+        load(m).wait()
+        for c in reversed(range(n_cell)):
+            first = pl.multiple_of(flip(cell, c) * width, 128)
+            block = (weight * stage[m, :, pl.ds(first, width)]).astype(jnp.bfloat16)
+            if m or c:
+                outgoing[m, c] = block
+            else:
+                rows[dp * n_cell + cell] = block
+            if place == 0 and c == n_cell - 1:
+                pl.semaphore_wait(barrier, n_dp * n_cell - 1)
+            if m or c:
+                transfer(m, c).start()
+
+    table = table_ref[...]
+    high = table.astype(jnp.bfloat16)
+    left = table - high.astype(jnp.float32)
+    middle = left.astype(jnp.bfloat16)
+    low = (left - middle.astype(jnp.float32)).astype(jnp.bfloat16)
+    t_rows, t_cols = table.shape
+    tile = min(width, 512)
+
+    @pl.loop(0, width // tile)
+    def _(i):
+        at = pl.ds(pl.multiple_of(i * tile, 128), tile)
+        where = perm_ref[:, at]
+        hit = (lax.broadcasted_iota(jnp.int32, (t_cols, tile), 0) == where % t_cols)
+        hit = jnp.where(hit, 1.0, 0.0).astype(jnp.bfloat16)
+        found = jnp.dot(high, hit, preferred_element_type=jnp.float32)
+        found = found + jnp.dot(middle, hit, preferred_element_type=jnp.float32)
+        found = found + jnp.dot(low, hit, preferred_element_type=jnp.float32)
+        mine = lax.broadcasted_iota(jnp.int32, (t_rows, tile), 0) == where // t_cols
+        column_var[:, at] = jnp.sum(jnp.where(mine, found, 0.0), axis=0, keepdims=True)
+
+    for m in range(n_dp):
+        group = flip(dp, m)
+        for c in range(n_cell):
+            if m or c:
+                arrival(m, c).wait_recv()
+
+        @pl.loop(0, n_cell)
+        def _(c):
+            block = rows[group * n_cell + c].astype(jnp.float32) * column_var[...]
+            weighted[group * n_cell + c] = block.astype(jnp.bfloat16)
+
+        def product(a, b):
+            left_rows = rows[pl.ds(a * n_cell, n_cell)].reshape(plane, width)
+            right_rows = weighted[pl.ds(b * n_cell, n_cell)].reshape(plane, width)
+            at_row = pl.ds(pl.multiple_of(a * plane, plane), plane)
+            at_col = pl.ds(pl.multiple_of(b * plane, plane), plane)
+            partial[at_row, at_col] = against(left_rows, right_rows)
+
+        product(group, group)
+        for other in range(m):
+            product(group, flip(dp, other))
+            product(flip(dp, other), group)
+
+    part = n_total // n_cell
+    index = 0
+    for steps in rounds:
+        pending = []
+        for bit, left_bits, half in steps:
+            n_cols = n_total if half is None else n_total // 2
+            cols = pl.ds(0 if half is None else half * n_cols, n_cols)
+            for slot, sub in enumerate(subsets(left_bits)):
+                there = pl.ds(pl.multiple_of(flip(cell, (1 << bit) ^ sub) * part, part), part)
+                here = pl.ds(pl.multiple_of(flip(cell, sub) * part, part), part)
+                copy = pltpu.make_async_remote_copy(
+                    src_ref=partial.at[there, cols],
+                    dst_ref=bufs[index].at[slot],
+                    send_sem=rs_send.at[index, slot],
+                    recv_sem=rs_recv.at[index, slot],
+                    device_id=(dp, flip(cell, 1 << bit)),
+                    device_id_type=MESH,
+                )
+                copy.start()
+                pending.append((copy, index, slot, here, cols))
+            index += 1
+        for copy, at, slot, here, cols in pending:
+            copy.wait_recv()
+            partial[here, cols] += bufs[at][slot]
+        for copy, *_ in pending:
+            copy.wait_send()
+
+    mine = pl.ds(pl.multiple_of(cell * part, part), part)
+    out_cols = n_total // n_dp
+
+    def columns_of(index):
+        return pl.ds(pl.multiple_of(index * out_cols, out_cols), out_cols)
+
+    last = []
+    for m in reversed(range(1, n_dp)):
+        copy = pltpu.make_async_remote_copy(
+            src_ref=partial.at[mine, columns_of(flip(dp, m))],
+            dst_ref=z_buf.at[m],
+            send_sem=z_send.at[m],
+            recv_sem=z_recv.at[m],
+            device_id=(flip(dp, m), cell),
+            device_id_type=MESH,
+        )
+        copy.start()
+        last.append((copy, m))
+    total = partial[mine, columns_of(dp)]
+    for copy, m in reversed(last):
+        copy.wait_recv()
+        total = total + z_buf[m]
+    out_ref[...] = total
+    for copy, m in last:
+        copy.wait_send()
+    for m in range(n_dp):
+        for c in range(n_cell):
+            if m or c:
+                transfer(m, c).wait_send()
+
+
+def body_vmem(sensitivity, row_period, row_site, period_err, site_err, cell_var, cell_perm):
+    n_dp, n_cell = lax.axis_size("dp"), lax.axis_size("cell")
+    n_rows, n_all = sensitivity.shape
+    width = n_all // (n_dp * n_cell)
+    n_total = n_rows * n_dp * n_cell
+    part = n_total // n_cell
+    weight = weigh_rows(row_period, row_site, period_err, site_err)[:, None]
+    me = lax.axis_index("dp") * n_cell + lax.axis_index("cell")
+    perm = lax.dynamic_slice_in_dim(cell_perm, me * width, width)[None, :]
+    t_cols = min(512, n_all)
+    table = cell_var.reshape(n_all // t_cols, t_cols)
+    bufs = []
+    for steps in halvings(n_cell):
+        for _, left_bits, half in steps:
+            n_cols = n_total if half is None else n_total // 2
+            bufs.append(pltpu.VMEM((1 << len(left_bits), part, n_cols), jnp.float32))
+    n_bufs, n_slots = len(bufs), n_cell // 2
+    vmem = pl.BlockSpec(memory_space=pltpu.VMEM)
+    return pl.pallas_call(
+        functools.partial(gram_kernel, n_dp, n_cell),
+        out_shape=jax.ShapeDtypeStruct((part, n_total // n_dp), jnp.float32),
+        in_specs=[pl.BlockSpec(memory_space=pl.ANY), vmem, vmem, vmem],
+        out_specs=vmem,
+        scratch_shapes=[
+            pltpu.VMEM((n_dp, n_rows, n_cell * width), jnp.float32),
+            pltpu.VMEM((n_dp, n_cell, n_rows, width), jnp.bfloat16),
+            pltpu.VMEM((n_dp * n_cell, n_rows, width), jnp.bfloat16),
+            pltpu.VMEM((n_dp * n_cell, n_rows, width), jnp.bfloat16),
+            pltpu.VMEM((1, width), jnp.float32),
+            pltpu.VMEM((n_total, n_total), jnp.float32),
+            *bufs,
+            pltpu.VMEM((n_dp, part, n_total // n_dp), jnp.float32),
+            pltpu.SemaphoreType.DMA((n_dp,)),
+            pltpu.SemaphoreType.DMA((n_dp, n_cell)),
+            pltpu.SemaphoreType.DMA((n_dp, n_cell)),
+            pltpu.SemaphoreType.DMA((n_bufs, n_slots)),
+            pltpu.SemaphoreType.DMA((n_bufs, n_slots)),
+            pltpu.SemaphoreType.DMA((n_dp,)),
+            pltpu.SemaphoreType.DMA((n_dp,)),
+        ],
+        compiler_params=pltpu.CompilerParams(
+            collective_id=0, has_side_effects=True, vmem_limit_bytes=VMEM_BUDGET
+        ),
+        cost_estimate=pl.CostEstimate(
+            flops=2 * n_total * n_total * width, bytes_accessed=4 * n_rows * n_all, transcendentals=0
+        ),
+    )(sensitivity, weight, perm, table)
+
+
+def is_power_of_two(n):
+    return n & (n - 1) == 0
+
+
+def body(*arrays):
+    sensitivity = arrays[0]
+    n_dp, n_cell = lax.axis_size("dp"), lax.axis_size("cell")
+    n_rows, n_all = sensitivity.shape
+    n_total = n_rows * n_dp * n_cell
+    need = (4 + 2 + 2 + 2) * n_rows * n_all + 2 * 4 * n_total * n_total
+    fits = need < VMEM_BUDGET and is_power_of_two(n_dp) and is_power_of_two(n_cell) and n_cell > 1
+    return (body_vmem if fits else body_general)(*arrays)
 
 
 def solution(mesh):

time: 407 us -> 153 us (0.38)
  waiting for transfers between devices: 274 us -> 0 us
  Pallas kernels: 0 us -> 145 us
  blocking collectives: 54.1 us -> 0 us
  local copies, waits for them, and re-layouts: 45.8 us -> 5.24 us
  between operations: 13.4 us -> 0.01 us
  matrix products: 12.5 us -> 0 us
  other arithmetic: 6.46 us -> 1.71 us
    all_gather x1 -> x0, waiting for transfers between devices: 240 us -> none  [body(): lax.all_gather(scaled, 'dp', axis=0, tiled=True)]
    pallas_call x0 -> x1, Pallas kernels: none -> 145 us  [body_vmem(): pl.pallas_call(functools.partial(gram_kernel, n_dp, n_cell), out_shape=ja...]
    all_to_all x1 -> x0, blocking collectives: 54.1 us -> none  [body(): lax.all_to_all(packed, 'cell', split_axis=1, concat_axis=0, tiled=True)]
    gather x1 -> x0, local copies, waits for them, and re-layouts: 45.5 us -> none  [weigh_columns(): column_var = cell_var[positions]]
    reduce_scatter x1 -> x0, waiting for transfers between devices: 34.4 us -> none  [body(): lax.psum_scatter(partial_value, 'cell', scatter_dimension=0, tiled=True)]
    dot_general x1 -> x0, matrix products: 12.5 us -> none  [against(): lax.dot_general(rows_block, weighted, (((1,), (1,)), ((), ())), preferred...]
  transfers between devices with their start and end apart: 2 -> 0, of which waited for: 2 -> 0; matrix products, arithmetic and copies ran while one was open for 11% -> 0% of each run, Pallas kernels for 0% -> 0%
where the time goes in v1:
time: 153 us; the launch traced here: 152 us
  Pallas kernels  145 us (95%)
  local copies, waits for them, and re-layouts  5.24 us (3%)
  other arithmetic  1.71 us (1%)
    pallas_call x1, Pallas kernels, body_vmem(): pl.pallas_call(functools.partial(gram_kernel, n_dp, n_cell), out_shape=ja...  145 us

profile of v1, /device:TPU:0, one launch (start us, length us, event | category | flops | bytes accessed | tf_op | source)
XLA Modules:
  0.0 152.2 jit_solution(16011972942635462420)
XLA Ops:
  0.0 0.8 select_reduce_fusion.1
  0.9 0.9 select_reduce_fusion
  1.7 1.3 dynamic_slice.3
  3.0 0.7 copy.9.weight_ref
  3.7 1.7 %reshape.31.table_ref = f32[128,512]{1,0:T(8,128)} reshape(f32[65536]{0:T(1024)} %param.12) | data formatting | bytes 524288 | tf_op jit(solution)/shard_map/reshape | solution.py:250
  5.4 145.2 %shard_map.73 = f32[128,256]{1,0:T(8,128)} custom-call(f32[32,65536]{1,0:T(8,128)} %sens_ref.1, f32[32,1]{1,0:T(8,128)} %copy.9.weight_ref, s32[1,2048]{1,0:T(1,128)} %bitcast.3, f32[128,512]{1,0:T(8,128)} %reshape.31.table_ref), custom_call_target="tpu_custom_call" | custom-call | flops 4294967296 | bytes 8388608 | tf_op jit(solution)/shard_map/pallas_call | solution.py:258
  150.6 1.6 %copy.11 = f32[128,256]{1,0:T(8,128)} copy(f32[128,256]{1,0:T(8,128)} %shard_map.73) | data formatting | bytes 262144
  (1 shorter events, 0.0 us)

commit v2 on v1

--- a/solution.py
+++ b/solution.py
@@ -8,6 +8,7 @@
 
 MESH = pl.DeviceIdType.MESH
 VMEM_BUDGET = 56 * 1024 * 1024
+PIECES = 4
 
 
 def weigh_rows(row_period, row_site, period_err, site_err):
@@ -63,14 +64,25 @@
     return masks
 
 
-def halvings(n_cell):
+def halvings(n_dp, n_cell):
     levels = n_cell.bit_length() - 1
     rest = list(range(1, levels))
     orders = (rest, rest[::-1])
-    rounds = [[(0, rest, None)]]
+    rounds = [[("cell", 0, rest, None, jnp.float32)]]
     for depth in range(len(rest)):
-        rounds.append([(order[depth], order[depth + 1:], half) for half, order in enumerate(orders)])
+        rounds.append([
+            ("cell", order[depth], order[depth + 1:], half, jnp.bfloat16) for half, order in enumerate(orders)
+        ])
+    dp_levels = n_dp.bit_length() - 1
+    for bit in range(dp_levels):
+        rounds.append([("dp", bit, list(range(bit + 1, dp_levels)), None, jnp.float32)])
     return rounds
+
+
+def step_shape(step, n_dp, n_cell, n_total):
+    axis, _, left_bits, half, _ = step
+    n_cols = n_total // n_dp if axis == "dp" else n_total if half is None else n_total // 2
+    return (PIECES, 1 << len(left_bits), n_total // n_cell // PIECES, n_cols)
 
 
 def gram_kernel(
@@ -78,15 +90,23 @@
     sens_ref, weight_ref, perm_ref, table_ref, out_ref,
     stage, outgoing, rows, weighted, column_var, partial, *rest,
 ):
-    rounds = halvings(n_cell)
-    n_bufs = sum(len(steps) for steps in rounds)
-    bufs, (z_buf, load_sem, send_sem, recv_sem, rs_send, rs_recv, z_send, z_recv) = rest[:n_bufs], rest[n_bufs:]
+    rounds = halvings(n_dp, n_cell)
+    flat = [step for steps in rounds for step in steps]
+    rest = list(rest)
+    arrived = [rest.pop(0) for _ in flat]
+    leaving = [rest.pop(0) if step[-1] != jnp.float32 else None for step in flat]
+    load_sem, send_sem, recv_sem, sum_send, sum_recv = rest
     dp, cell = lax.axis_index("dp"), lax.axis_index("cell")
     n_rows, n_all = sens_ref.shape
     width = n_all // (n_dp * n_cell)
     plane = n_cell * n_rows
     n_total = n_dp * plane
-    send_order = sorted(range(n_dp), key=lambda m: (m == 0, -m))
+    top = n_dp // 2
+    early = [m for m in reversed(range(n_dp)) if m != top]
+    send_order = [(m, c) for c in reversed(range(n_cell)) for m in early]
+    if top:
+        send_order += [(top, c) for c in reversed(range(n_cell))]
+    group_order = sorted(range(n_dp), key=lambda m: (m == top, m))
 
     barrier = pltpu.get_barrier_semaphore()
     for m in range(n_dp):
@@ -94,12 +114,12 @@
             if m or c:
                 pl.semaphore_signal(barrier, inc=1, device_id=(flip(dp, m), flip(cell, c)), device_id_type=MESH)
 
-    def load(m):
-        first = pl.multiple_of(flip(dp, m) * (n_cell * width), 128)
-        return pltpu.make_async_copy(sens_ref.at[:, pl.ds(first, n_cell * width)], stage.at[m], load_sem.at[m])
-
-    for m in send_order:
-        load(m).start()
+    def load(m, c):
+        first = pl.multiple_of((flip(dp, m) * n_cell + flip(cell, c)) * width, 128)
+        return pltpu.make_async_copy(sens_ref.at[:, pl.ds(first, width)], stage.at[m, c], load_sem.at[m, c])
+
+    for m, c in send_order:
+        load(m, c).start()
 
     def transfer(m, c):
         return pltpu.make_async_remote_copy(
@@ -122,19 +142,17 @@
         )
 
     weight = weight_ref[...]
-    for place, m in enumerate(send_order):
-        load(m).wait()
-        for c in reversed(range(n_cell)):
-            first = pl.multiple_of(flip(cell, c) * width, 128)
-            block = (weight * stage[m, :, pl.ds(first, width)]).astype(jnp.bfloat16)
-            if m or c:
-                outgoing[m, c] = block
-            else:
-                rows[dp * n_cell + cell] = block
-            if place == 0 and c == n_cell - 1:
-                pl.semaphore_wait(barrier, n_dp * n_cell - 1)
-            if m or c:
-                transfer(m, c).start()
+    for place, (m, c) in enumerate(send_order):
+        load(m, c).wait()
+        block = (weight * stage[m, c]).astype(jnp.bfloat16)
+        if m or c:
+            outgoing[m, c] = block
+        else:
+            rows[dp * n_cell + cell] = block
+        if place == 0:
+            pl.semaphore_wait(barrier, n_dp * n_cell - 1)
+        if m or c:
+            transfer(m, c).start()
 
     table = table_ref[...]
     high = table.astype(jnp.bfloat16)
@@ -156,7 +174,7 @@
         mine = lax.broadcasted_iota(jnp.int32, (t_rows, tile), 0) == where // t_cols
         column_var[:, at] = jnp.sum(jnp.where(mine, found, 0.0), axis=0, keepdims=True)
 
-    for m in range(n_dp):
+    for place, m in enumerate(group_order):
         group = flip(dp, m)
         for c in range(n_cell):
             if m or c:
@@ -175,62 +193,76 @@
             partial[at_row, at_col] = against(left_rows, right_rows)
 
         product(group, group)
-        for other in range(m):
+        for other in group_order[:place]:
             product(group, flip(dp, other))
             product(flip(dp, other), group)
 
-    part = n_total // n_cell
-    index = 0
+    part, out_cols = n_total // n_cell, n_total // n_dp
+    piece_rows = part // PIECES
+    numbers, count = [], 0
     for steps in rounds:
-        pending = []
-        for bit, left_bits, half in steps:
-            n_cols = n_total if half is None else n_total // 2
-            cols = pl.ds(0 if half is None else half * n_cols, n_cols)
-            for slot, sub in enumerate(subsets(left_bits)):
-                there = pl.ds(pl.multiple_of(flip(cell, (1 << bit) ^ sub) * part, part), part)
-                here = pl.ds(pl.multiple_of(flip(cell, sub) * part, part), part)
-                copy = pltpu.make_async_remote_copy(
-                    src_ref=partial.at[there, cols],
-                    dst_ref=bufs[index].at[slot],
-                    send_sem=rs_send.at[index, slot],
-                    recv_sem=rs_recv.at[index, slot],
-                    device_id=(dp, flip(cell, 1 << bit)),
-                    device_id_type=MESH,
-                )
-                copy.start()
-                pending.append((copy, index, slot, here, cols))
-            index += 1
-        for copy, at, slot, here, cols in pending:
-            copy.wait_recv()
-            partial[here, cols] += bufs[at][slot]
-        for copy, *_ in pending:
-            copy.wait_send()
-
-    mine = pl.ds(pl.multiple_of(cell * part, part), part)
-    out_cols = n_total // n_dp
+        numbers.append(list(range(count, count + len(steps))))
+        count += len(steps)
+
+    def rows_of(block, piece):
+        return pl.ds(pl.multiple_of(block * part + piece * piece_rows, piece_rows), piece_rows)
 
     def columns_of(index):
         return pl.ds(pl.multiple_of(index * out_cols, out_cols), out_cols)
 
-    last = []
-    for m in reversed(range(1, n_dp)):
-        copy = pltpu.make_async_remote_copy(
-            src_ref=partial.at[mine, columns_of(flip(dp, m))],
-            dst_ref=z_buf.at[m],
-            send_sem=z_send.at[m],
-            recv_sem=z_recv.at[m],
-            device_id=(flip(dp, m), cell),
-            device_id_type=MESH,
-        )
-        copy.start()
-        last.append((copy, m))
-    total = partial[mine, columns_of(dp)]
-    for copy, m in reversed(last):
-        copy.wait_recv()
-        total = total + z_buf[m]
-    out_ref[...] = total
-    for copy, m in last:
-        copy.wait_send()
+    def exchanges(number, piece):
+        axis, bit, left_bits, half, kind = flat[number]
+        found = []
+        for slot, sub in enumerate(subsets(left_bits)):
+            if axis == "cell":
+                n_cols = n_total if half is None else n_total // 2
+                cols = pl.ds(0 if half is None else half * n_cols, n_cols)
+                there = (rows_of(flip(cell, (1 << bit) ^ sub), piece), cols)
+                here = (rows_of(flip(cell, sub), piece), cols)
+                device = (dp, flip(cell, 1 << bit))
+            else:
+                mine = rows_of(cell, piece)
+                there = (mine, columns_of(flip(dp, (1 << bit) ^ sub)))
+                here = (mine, columns_of(flip(dp, sub)))
+                device = (flip(dp, 1 << bit), cell)
+            source = partial.at[there] if kind == jnp.float32 else leaving[number].at[piece, slot]
+            copy = pltpu.make_async_remote_copy(
+                src_ref=source,
+                dst_ref=arrived[number].at[piece, slot],
+                send_sem=sum_send.at[number, piece, slot],
+                recv_sem=sum_recv.at[number, piece, slot],
+                device_id=device,
+                device_id_type=MESH,
+            )
+            found.append((copy, slot, there, here))
+        return found
+
+    def begin(steps, piece):
+        for number in steps:
+            for copy, slot, there, _ in exchanges(number, piece):
+                if leaving[number] is not None:
+                    leaving[number][piece, slot] = partial[there].astype(leaving[number].dtype)
+                copy.start()
+
+    def finish(steps, piece):
+        for number in steps:
+            for copy, slot, _, here in exchanges(number, piece):
+                copy.wait_recv()
+                partial[here] += arrived[number][piece, slot].astype(jnp.float32)
+
+    for depth, steps in enumerate(numbers):
+        for piece in range(PIECES):
+            if depth:
+                finish(numbers[depth - 1], piece)
+            begin(steps, piece)
+    for piece in range(PIECES):
+        finish(numbers[-1], piece)
+        out_ref[pl.ds(piece * piece_rows, piece_rows)] = partial[rows_of(cell, piece), columns_of(dp)]
+
+    for number in range(count):
+        for piece in range(PIECES):
+            for copy, *_ in exchanges(number, piece):
+                copy.wait_send()
     for m in range(n_dp):
         for c in range(n_cell):
             if m or c:
@@ -248,12 +280,12 @@
     perm = lax.dynamic_slice_in_dim(cell_perm, me * width, width)[None, :]
     t_cols = min(512, n_all)
     table = cell_var.reshape(n_all // t_cols, t_cols)
-    bufs = []
-    for steps in halvings(n_cell):
-        for _, left_bits, half in steps:
-            n_cols = n_total if half is None else n_total // 2
-            bufs.append(pltpu.VMEM((1 << len(left_bits), part, n_cols), jnp.float32))
-    n_bufs, n_slots = len(bufs), n_cell // 2
+    flat = [step for steps in halvings(n_dp, n_cell) for step in steps]
+    bufs = [pltpu.VMEM(step_shape(step, n_dp, n_cell, n_total), step[-1]) for step in flat]
+    bufs += [
+        pltpu.VMEM(step_shape(step, n_dp, n_cell, n_total), step[-1]) for step in flat if step[-1] != jnp.float32
+    ]
+    sums = (len(flat), PIECES, n_cell // 2 + n_dp // 2)
     vmem = pl.BlockSpec(memory_space=pltpu.VMEM)
     return pl.pallas_call(
         functools.partial(gram_kernel, n_dp, n_cell),
@@ -261,21 +293,18 @@
         in_specs=[pl.BlockSpec(memory_space=pl.ANY), vmem, vmem, vmem],
         out_specs=vmem,
         scratch_shapes=[
-            pltpu.VMEM((n_dp, n_rows, n_cell * width), jnp.float32),
+            pltpu.VMEM((n_dp, n_cell, n_rows, width), jnp.float32),
             pltpu.VMEM((n_dp, n_cell, n_rows, width), jnp.bfloat16),
             pltpu.VMEM((n_dp * n_cell, n_rows, width), jnp.bfloat16),
             pltpu.VMEM((n_dp * n_cell, n_rows, width), jnp.bfloat16),
             pltpu.VMEM((1, width), jnp.float32),
             pltpu.VMEM((n_total, n_total), jnp.float32),
             *bufs,
-            pltpu.VMEM((n_dp, part, n_total // n_dp), jnp.float32),
-            pltpu.SemaphoreType.DMA((n_dp,)),
             pltpu.SemaphoreType.DMA((n_dp, n_cell)),
             pltpu.SemaphoreType.DMA((n_dp, n_cell)),
-            pltpu.SemaphoreType.DMA((n_bufs, n_slots)),
-            pltpu.SemaphoreType.DMA((n_bufs, n_slots)),
-            pltpu.SemaphoreType.DMA((n_dp,)),
-            pltpu.SemaphoreType.DMA((n_dp,)),
+            pltpu.SemaphoreType.DMA((n_dp, n_cell)),
+            pltpu.SemaphoreType.DMA(sums),
+            pltpu.SemaphoreType.DMA(sums),
         ],
         compiler_params=pltpu.CompilerParams(
             collective_id=0, has_side_effects=True, vmem_limit_bytes=VMEM_BUDGET
@@ -296,7 +325,7 @@
     n_rows, n_all = sensitivity.shape
     n_total = n_rows * n_dp * n_cell
     need = (4 + 2 + 2 + 2) * n_rows * n_all + 2 * 4 * n_total * n_total
-    fits = need < VMEM_BUDGET and is_power_of_two(n_dp) and is_power_of_two(n_cell) and n_cell > 1
+    fits = n_total // n_cell % (16 * PIECES) == 0 and need < VMEM_BUDGET and is_power_of_two(n_dp) and is_power_of_two(n_cell) and n_cell > 1
     return (body_vmem if fits else body_general)(*arrays)
 
 

time: 153 us -> 142 us (0.928)
  Pallas kernels: 145 us -> 135 us
    pallas_call x1, Pallas kernels: 145 us -> 135 us  [body_vmem(): pl.pallas_call(functools.partial(gram_kernel, n_dp, n_cell), out_shape=ja...]
where the time goes in v2:
time: 142 us
  Pallas kernels  135 us (95%)
  local copies, waits for them, and re-layouts  5.24 us (4%)
  other arithmetic  1.71 us (1%)
    pallas_call x1, Pallas kernels, body_vmem(): pl.pallas_call(functools.partial(gram_kernel, n_dp, n_cell), out_shape=ja...  135 us

profile of v2, /device:TPU:0, one launch (start us, length us, event | category | flops | bytes accessed | tf_op | source)
XLA Modules:
  0.0 142.2 jit_solution(4280070752706797716)
XLA Ops:
  0.0 0.8 select_reduce_fusion.1
  0.9 0.9 select_reduce_fusion
  1.7 1.3 dynamic_slice.3
  3.0 0.7 copy.9.weight_ref
  3.7 1.7 %reshape.31.table_ref = f32[128,512]{1,0:T(8,128)} reshape(f32[65536]{0:T(1024)} %param.12) | data formatting | bytes 524288 | tf_op jit(solution)/shard_map/reshape | solution.py:282
  5.4 135.2 %shard_map.73 = f32[128,256]{1,0:T(8,128)} custom-call(f32[32,65536]{1,0:T(8,128)} %sens_ref.1, f32[32,1]{1,0:T(8,128)} %copy.9.weight_ref, s32[1,2048]{1,0:T(1,128)} %bitcast.3, f32[128,512]{1,0:T(8,128)} %reshape.31.table_ref), custom_call_target="tpu_custom_call" | custom-call | flops 4294967296 | bytes 8388608 | tf_op jit(solution)/shard_map/pallas_call | solution.py:290
  140.6 1.6 %copy.11 = f32[128,256]{1,0:T(8,128)} copy(f32[128,256]{1,0:T(8,128)} %shard_map.73) | data formatting | bytes 262144
  (1 shorter events, 0.0 us)

commit v3 on v2

--- a/solution.py
+++ b/solution.py
@@ -9,6 +9,7 @@
 MESH = pl.DeviceIdType.MESH
 VMEM_BUDGET = 56 * 1024 * 1024
 PIECES = 4
+CHUNKS = 4
 
 
 def weigh_rows(row_period, row_site, period_err, site_err):
@@ -71,7 +72,7 @@
     rounds = [[("cell", 0, rest, None, jnp.float32)]]
     for depth in range(len(rest)):
         rounds.append([
-            ("cell", order[depth], order[depth + 1:], half, jnp.bfloat16) for half, order in enumerate(orders)
+            ("cell", order[depth], order[depth + 1:], half, jnp.float32) for half, order in enumerate(orders)
         ])
     dp_levels = n_dp.bit_length() - 1
     for bit in range(dp_levels):
@@ -87,26 +88,25 @@
 
 def gram_kernel(
     n_dp, n_cell,
-    sens_ref, weight_ref, perm_ref, table_ref, out_ref,
-    stage, outgoing, rows, weighted, column_var, partial, *rest,
+    sens_ref, weight_ref, perm_ref, var_ref, out_ref,
+    stage, outgoing, rows, weighted, perm, flat_table, table, column_var, partial, *rest,
 ):
     rounds = halvings(n_dp, n_cell)
     flat = [step for steps in rounds for step in steps]
     rest = list(rest)
     arrived = [rest.pop(0) for _ in flat]
     leaving = [rest.pop(0) if step[-1] != jnp.float32 else None for step in flat]
-    load_sem, send_sem, recv_sem, sum_send, sum_recv = rest
+    load_sem, small_sem, send_sem, recv_sem, sum_send, sum_recv = rest
     dp, cell = lax.axis_index("dp"), lax.axis_index("cell")
     n_rows, n_all = sens_ref.shape
     width = n_all // (n_dp * n_cell)
     plane = n_cell * n_rows
     n_total = n_dp * plane
-    top = n_dp // 2
-    early = [m for m in reversed(range(n_dp)) if m != top]
-    send_order = [(m, c) for c in reversed(range(n_cell)) for m in early]
-    if top:
-        send_order += [(top, c) for c in reversed(range(n_cell))]
-    group_order = sorted(range(n_dp), key=lambda m: (m == top, m))
+    chunk_width = width // CHUNKS
+    far = [m for m in reversed(range(n_dp)) if m >= n_dp // 2]
+    near = [m for m in reversed(range(n_dp)) if m < n_dp // 2]
+    masks = [m for pair in zip(far, near) for m in pair] if near else far
+    send_order = [(m, c) for c in reversed(range(n_cell)) for m in masks]
 
     barrier = pltpu.get_barrier_semaphore()
     for m in range(n_dp):
@@ -120,82 +120,100 @@
 
     for m, c in send_order:
         load(m, c).start()
-
-    def transfer(m, c):
+    me = dp * n_cell + cell
+    load_perm = pltpu.make_async_copy(
+        perm_ref.at[pl.ds(pl.multiple_of(me * width, width), width)], perm, small_sem.at[0]
+    )
+    load_var = pltpu.make_async_copy(var_ref, flat_table, small_sem.at[1])
+    load_perm.start()
+    load_var.start()
+
+    def transfer(chunk, m, c):
         return pltpu.make_async_remote_copy(
-            src_ref=outgoing.at[m, c],
-            dst_ref=rows.at[dp * n_cell + cell],
-            send_sem=send_sem.at[m, c],
-            recv_sem=recv_sem.at[m, c],
+            src_ref=outgoing.at[chunk, m, c],
+            dst_ref=rows.at[chunk, me],
+            send_sem=send_sem.at[chunk, m, c],
+            recv_sem=recv_sem.at[chunk, m, c],
             device_id=(flip(dp, m), flip(cell, c)),
             device_id_type=MESH,
         )
 
-    def arrival(m, c):
+    def arrival(chunk, m, c):
         return pltpu.make_async_remote_copy(
-            src_ref=outgoing.at[m, c],
-            dst_ref=rows.at[flip(dp, m) * n_cell + flip(cell, c)],
-            send_sem=send_sem.at[m, c],
-            recv_sem=recv_sem.at[m, c],
+            src_ref=outgoing.at[chunk, m, c],
+            dst_ref=rows.at[chunk, flip(dp, m) * n_cell + flip(cell, c)],
+            send_sem=send_sem.at[chunk, m, c],
+            recv_sem=recv_sem.at[chunk, m, c],
             device_id=(flip(dp, m), flip(cell, c)),
             device_id_type=MESH,
         )
 
     weight = weight_ref[...]
-    for place, (m, c) in enumerate(send_order):
-        load(m, c).wait()
-        block = (weight * stage[m, c]).astype(jnp.bfloat16)
-        if m or c:
-            outgoing[m, c] = block
-        else:
-            rows[dp * n_cell + cell] = block
-        if place == 0:
-            pl.semaphore_wait(barrier, n_dp * n_cell - 1)
-        if m or c:
-            transfer(m, c).start()
-
-    table = table_ref[...]
-    high = table.astype(jnp.bfloat16)
-    left = table - high.astype(jnp.float32)
+    for chunk in range(CHUNKS):
+        for place, (m, c) in enumerate(send_order):
+            if chunk == 0:
+                load(m, c).wait()
+            at = pl.ds(chunk * chunk_width, chunk_width)
+            block = (weight * stage[m, c, :, at]).astype(jnp.bfloat16)
+            if m or c:
+                outgoing[chunk, m, c] = block
+            else:
+                rows[chunk, me] = block
+            if chunk == 0 and place == 0:
+                pl.semaphore_wait(barrier, n_dp * n_cell - 1)
+            if m or c:
+                transfer(chunk, m, c).start()
+
+    load_perm.wait()
+    load_var.wait()
+    t_rows, t_cols = table.shape
+
+    @pl.loop(0, t_rows)
+    def _(i):
+        at = pl.ds(pl.multiple_of(i * t_cols, t_cols), t_cols)
+        table[pl.ds(i, 1), :] = flat_table[at].reshape(1, t_cols)
+
+    values = table[...]
+    high = values.astype(jnp.bfloat16)
+    left = values - high.astype(jnp.float32)
     middle = left.astype(jnp.bfloat16)
     low = (left - middle.astype(jnp.float32)).astype(jnp.bfloat16)
-    t_rows, t_cols = table.shape
-    tile = min(width, 512)
+    tile = chunk_width
 
     @pl.loop(0, width // tile)
     def _(i):
-        at = pl.ds(pl.multiple_of(i * tile, 128), tile)
-        where = perm_ref[:, at]
+        at = pl.ds(pl.multiple_of(i * tile, tile), tile)
+        where = perm[at].reshape(1, tile)
         hit = (lax.broadcasted_iota(jnp.int32, (t_cols, tile), 0) == where % t_cols)
         hit = jnp.where(hit, 1.0, 0.0).astype(jnp.bfloat16)
         found = jnp.dot(high, hit, preferred_element_type=jnp.float32)
         found = found + jnp.dot(middle, hit, preferred_element_type=jnp.float32)
         found = found + jnp.dot(low, hit, preferred_element_type=jnp.float32)
         mine = lax.broadcasted_iota(jnp.int32, (t_rows, tile), 0) == where // t_cols
-        column_var[:, at] = jnp.sum(jnp.where(mine, found, 0.0), axis=0, keepdims=True)
-
-    for place, m in enumerate(group_order):
-        group = flip(dp, m)
-        for c in range(n_cell):
-            if m or c:
-                arrival(m, c).wait_recv()
-
-        @pl.loop(0, n_cell)
-        def _(c):
-            block = rows[group * n_cell + c].astype(jnp.float32) * column_var[...]
-            weighted[group * n_cell + c] = block.astype(jnp.bfloat16)
-
-        def product(a, b):
-            left_rows = rows[pl.ds(a * n_cell, n_cell)].reshape(plane, width)
-            right_rows = weighted[pl.ds(b * n_cell, n_cell)].reshape(plane, width)
-            at_row = pl.ds(pl.multiple_of(a * plane, plane), plane)
-            at_col = pl.ds(pl.multiple_of(b * plane, plane), plane)
-            partial[at_row, at_col] = against(left_rows, right_rows)
-
-        product(group, group)
-        for other in group_order[:place]:
-            product(group, flip(dp, other))
-            product(flip(dp, other), group)
+        column_var[i] = jnp.sum(jnp.where(mine, found, 0.0), axis=0, keepdims=True)
+
+    for chunk in range(CHUNKS):
+        for m, c in send_order:
+            if m or c:
+                arrival(chunk, m, c).wait_recv()
+
+        @pl.loop(0, n_dp)
+        def _(group):
+            first = group * n_cell
+
+            @pl.loop(0, n_cell)
+            def _(c):
+                block = rows[chunk, first + c].astype(jnp.float32) * column_var[chunk]
+                weighted[first + c] = block.astype(jnp.bfloat16)
+
+            right_rows = weighted[pl.ds(first, n_cell)].reshape(plane, chunk_width)
+            left_rows = rows[chunk].reshape(n_total, chunk_width)
+            cols = pl.ds(pl.multiple_of(group * plane, plane), plane)
+            term = against(left_rows, right_rows)
+            if chunk == 0:
+                partial[:, cols] = term
+            else:
+                partial[:, cols] += term
 
     part, out_cols = n_total // n_cell, n_total // n_dp
     piece_rows = part // PIECES
@@ -263,10 +281,10 @@
         for piece in range(PIECES):
             for copy, *_ in exchanges(number, piece):
                 copy.wait_send()
-    for m in range(n_dp):
-        for c in range(n_cell):
-            if m or c:
-                transfer(m, c).wait_send()
+    for chunk in range(CHUNKS):
+        for m, c in send_order:
+            if m or c:
+                transfer(chunk, m, c).wait_send()
 
 
 def body_vmem(sensitivity, row_period, row_site, period_err, site_err, cell_var, cell_perm):
@@ -276,33 +294,35 @@
     n_total = n_rows * n_dp * n_cell
     part = n_total // n_cell
     weight = weigh_rows(row_period, row_site, period_err, site_err)[:, None]
-    me = lax.axis_index("dp") * n_cell + lax.axis_index("cell")
-    perm = lax.dynamic_slice_in_dim(cell_perm, me * width, width)[None, :]
     t_cols = min(512, n_all)
-    table = cell_var.reshape(n_all // t_cols, t_cols)
     flat = [step for steps in halvings(n_dp, n_cell) for step in steps]
     bufs = [pltpu.VMEM(step_shape(step, n_dp, n_cell, n_total), step[-1]) for step in flat]
     bufs += [
         pltpu.VMEM(step_shape(step, n_dp, n_cell, n_total), step[-1]) for step in flat if step[-1] != jnp.float32
     ]
     sums = (len(flat), PIECES, n_cell // 2 + n_dp // 2)
-    vmem = pl.BlockSpec(memory_space=pltpu.VMEM)
+    hbm, vmem = pl.BlockSpec(memory_space=pl.ANY), pl.BlockSpec(memory_space=pltpu.VMEM)
+    chunk_width = width // CHUNKS
     return pl.pallas_call(
         functools.partial(gram_kernel, n_dp, n_cell),
         out_shape=jax.ShapeDtypeStruct((part, n_total // n_dp), jnp.float32),
-        in_specs=[pl.BlockSpec(memory_space=pl.ANY), vmem, vmem, vmem],
+        in_specs=[hbm, vmem, hbm, hbm],
         out_specs=vmem,
         scratch_shapes=[
             pltpu.VMEM((n_dp, n_cell, n_rows, width), jnp.float32),
-            pltpu.VMEM((n_dp, n_cell, n_rows, width), jnp.bfloat16),
-            pltpu.VMEM((n_dp * n_cell, n_rows, width), jnp.bfloat16),
-            pltpu.VMEM((n_dp * n_cell, n_rows, width), jnp.bfloat16),
-            pltpu.VMEM((1, width), jnp.float32),
+            pltpu.VMEM((CHUNKS, n_dp, n_cell, n_rows, chunk_width), jnp.bfloat16),
+            pltpu.VMEM((CHUNKS, n_dp * n_cell, n_rows, chunk_width), jnp.bfloat16),
+            pltpu.VMEM((n_dp * n_cell, n_rows, chunk_width), jnp.bfloat16),
+            pltpu.VMEM((width,), jnp.int32),
+            pltpu.VMEM((n_all,), jnp.float32),
+            pltpu.VMEM((n_all // t_cols, t_cols), jnp.float32),
+            pltpu.VMEM((CHUNKS, 1, chunk_width), jnp.float32),
             pltpu.VMEM((n_total, n_total), jnp.float32),
             *bufs,
             pltpu.SemaphoreType.DMA((n_dp, n_cell)),
-            pltpu.SemaphoreType.DMA((n_dp, n_cell)),
-            pltpu.SemaphoreType.DMA((n_dp, n_cell)),
+            pltpu.SemaphoreType.DMA((2,)),
+            pltpu.SemaphoreType.DMA((CHUNKS, n_dp, n_cell)),
+            pltpu.SemaphoreType.DMA((CHUNKS, n_dp, n_cell)),
             pltpu.SemaphoreType.DMA(sums),
             pltpu.SemaphoreType.DMA(sums),
         ],
@@ -312,7 +332,7 @@
         cost_estimate=pl.CostEstimate(
             flops=2 * n_total * n_total * width, bytes_accessed=4 * n_rows * n_all, transcendentals=0
         ),
-    )(sensitivity, weight, perm, table)
+    )(sensitivity, weight, cell_perm, cell_var)
 
 
 def is_power_of_two(n):
@@ -325,7 +345,8 @@
     n_rows, n_all = sensitivity.shape
     n_total = n_rows * n_dp * n_cell
     need = (4 + 2 + 2 + 2) * n_rows * n_all + 2 * 4 * n_total * n_total
-    fits = n_total // n_cell % (16 * PIECES) == 0 and need < VMEM_BUDGET and is_power_of_two(n_dp) and is_power_of_two(n_cell) and n_cell > 1
+    width = n_all // (n_dp * n_cell)
+    fits = n_total // n_cell % (16 * PIECES) == 0 and width % (128 * CHUNKS) == 0 and need < VMEM_BUDGET and is_power_of_two(n_dp) and is_power_of_two(n_cell) and n_cell > 1
     return (body_vmem if fits else body_general)(*arrays)
 
 

time: 142 us -> 141 us (level)
  local copies, waits for them, and re-layouts: 5.24 us -> 2.27 us
  Pallas kernels: 135 us -> 137 us
    reshape x1 -> x0, local copies, waits for them, and re-layouts: 1.68 us -> none  [body_vmem(): table = cell_var.reshape(n_all // t_cols, t_cols)]
    pallas_call x1, Pallas kernels: 135 us -> 137 us  [body_vmem(): pl.pallas_call(functools.partial(gram_kernel, n_dp, n_cell), out_shape=ja...]
where the time goes in v3:
time: 141 us
  Pallas kernels  137 us (97%)
  local copies, waits for them, and re-layouts  2.27 us (2%)
  other arithmetic  1.71 us (1%)
    pallas_call x1, Pallas kernels, body_vmem(): pl.pallas_call(functools.partial(gram_kernel, n_dp, n_cell), out_shape=ja...  137 us

profile of v3, /device:TPU:0, one launch (start us, length us, event | category | flops | bytes accessed | tf_op | source)
XLA Modules:
  0.0 140.8 jit_solution(7228302749641568160)
XLA Ops:
  0.0 0.8 select_reduce_fusion.1
  0.9 0.9 select_reduce_fusion
  1.7 0.7 copy.9.weight_ref
  2.4 136.8 %shard_map.73 = f32[128,256]{1,0:T(8,128)} custom-call(f32[32,65536]{1,0:T(8,128)} %sens_ref.1, f32[32,1]{1,0:T(8,128)} %copy.9.weight_ref, s32[65536]{0:T(1024)} %perm_ref.1, f32[65536]{0:T(1024)} %var_ref.1), custom_call_target="tpu_custom_call" | custom-call | flops 4294967296 | bytes 8388608 | tf_op jit(solution)/shard_map/pallas_call | solution.py:306
  139.2 1.6 %copy.11 = f32[128,256]{1,0:T(8,128)} copy(f32[128,256]{1,0:T(8,128)} %shard_map.73) | data formatting | bytes 262144
  (1 shorter events, 0.0 us)

commit v4 on v3

--- a/solution.py
+++ b/solution.py
@@ -88,7 +88,7 @@
 
 def gram_kernel(
     n_dp, n_cell,
-    sens_ref, weight_ref, perm_ref, var_ref, out_ref,
+    sens_ref, period_ref, site_ref, period_err_ref, site_err_ref, perm_ref, var_ref, out_ref,
     stage, outgoing, rows, weighted, perm, flat_table, table, column_var, partial, *rest,
 ):
     rounds = halvings(n_dp, n_cell)
@@ -106,7 +106,8 @@
     far = [m for m in reversed(range(n_dp)) if m >= n_dp // 2]
     near = [m for m in reversed(range(n_dp)) if m < n_dp // 2]
     masks = [m for pair in zip(far, near) for m in pair] if near else far
-    send_order = [(m, c) for c in reversed(range(n_cell)) for m in masks]
+    spread = [c for low in range(n_cell // 2) for c in (n_cell - 1 - low, low)]
+    send_order = [(m, c if m in far else n_cell - 1 - c) for c in spread for m in masks]
 
     barrier = pltpu.get_barrier_semaphore()
     for m in range(n_dp):
@@ -148,7 +149,19 @@
             device_id_type=MESH,
         )
 
-    weight = weight_ref[...]
+    diagonal = lax.broadcasted_iota(jnp.int32, (n_rows, n_rows), 0) == lax.broadcasted_iota(
+        jnp.int32, (n_rows, n_rows), 1
+    )
+
+    def look_up(index_ref, err_ref):
+        n_err = err_ref.shape[0]
+        index = index_ref[...].reshape(1, n_rows).astype(jnp.float32)
+        index = jnp.sum(jnp.where(diagonal, index, 0.0), axis=1, keepdims=True).astype(jnp.int32)
+        hit = lax.broadcasted_iota(jnp.int32, (n_rows, n_err), 1) == index
+        return jnp.sum(jnp.where(hit, err_ref[...].reshape(1, n_err), 0.0), axis=1, keepdims=True)
+
+    period_scale, site_scale = look_up(period_ref, period_err_ref), look_up(site_ref, site_err_ref)
+    weight = 1.0 / jnp.sqrt(period_scale * period_scale + site_scale * site_scale)
     for chunk in range(CHUNKS):
         for place, (m, c) in enumerate(send_order):
             if chunk == 0:
@@ -293,7 +306,6 @@
     width = n_all // (n_dp * n_cell)
     n_total = n_rows * n_dp * n_cell
     part = n_total // n_cell
-    weight = weigh_rows(row_period, row_site, period_err, site_err)[:, None]
     t_cols = min(512, n_all)
     flat = [step for steps in halvings(n_dp, n_cell) for step in steps]
     bufs = [pltpu.VMEM(step_shape(step, n_dp, n_cell, n_total), step[-1]) for step in flat]
@@ -306,7 +318,7 @@
     return pl.pallas_call(
         functools.partial(gram_kernel, n_dp, n_cell),
         out_shape=jax.ShapeDtypeStruct((part, n_total // n_dp), jnp.float32),
-        in_specs=[hbm, vmem, hbm, hbm],
+        in_specs=[hbm, vmem, vmem, vmem, vmem, hbm, hbm],
         out_specs=vmem,
         scratch_shapes=[
             pltpu.VMEM((n_dp, n_cell, n_rows, width), jnp.float32),
@@ -332,7 +344,7 @@
         cost_estimate=pl.CostEstimate(
             flops=2 * n_total * n_total * width, bytes_accessed=4 * n_rows * n_all, transcendentals=0
         ),
-    )(sensitivity, weight, cell_perm, cell_var)
+    )(sensitivity, row_period, row_site, period_err, site_err, cell_perm, cell_var)
 
 
 def is_power_of_two(n):

time: 141 us -> 139 us (0.986)
  other arithmetic: 1.71 us -> 0 us
    reduce_sum x2 -> x0, other arithmetic: 1.7 us -> none  [the longest x1 0.85 us: weigh_rows(): site_scale = jnp.sum(jnp.where(site_hit, site_err[None, :], 0.0), axis=1)]
where the time goes in v4:
time: 139 us
  Pallas kernels  137 us (99%)
  local copies, waits for them, and re-layouts  1.57 us (1%)
    pallas_call x1, Pallas kernels, body_vmem(): pl.pallas_call(functools.partial(gram_kernel, n_dp, n_cell), out_shape=ja...  137 us

profile of v4, /device:TPU:0, one launch (start us, length us, event | category | flops | bytes accessed | tf_op | source)
XLA Modules:
  0.0 138.9 jit_solution(7586945261986661698)
XLA Ops:
  0.0 137.3 %shard_map.73 = f32[128,256]{1,0:T(8,128)} custom-call(f32[32,65536]{1,0:T(8,128)} %sens_ref.1, s32[32]{0:T(128)} %period_ref.1, s32[32]{0:T(128)} %site_ref.1, f32[32]{0:T(128)} %period_err_ref.1, f32[128]{0:T(128)} %site_err_ref.1, s32[65536]{0:T(1024)} %perm_ref.1, f32[65536]{0:T(1024)} %var_ref.1), custom_call_target="tpu_custom_call" | custom-call | flops 4294967296 | bytes 8388608 | tf_op jit(solution)/shard_map/pallas_call | solution.py:318
  137.4 1.6 %copy.9 = f32[128,256]{1,0:T(8,128)} copy(f32[128,256]{1,0:T(8,128)} %shard_map.73) | data formatting | bytes 262144

commit v5 on v4

--- a/solution.py
+++ b/solution.py
@@ -8,7 +8,7 @@
 
 MESH = pl.DeviceIdType.MESH
 VMEM_BUDGET = 56 * 1024 * 1024
-PIECES = 4
+PIECES = 2
 CHUNKS = 4
 
 

time: 139 us -> 139 us (level)
  no operation moved by 1% of the time
where the time goes in v5:
time: 139 us
  Pallas kernels  137 us (99%)
  local copies, waits for them, and re-layouts  1.57 us (1%)
    pallas_call x1, Pallas kernels, body_vmem(): pl.pallas_call(functools.partial(gram_kernel, n_dp, n_cell), out_shape=ja...  137 us

profile of v5, /device:TPU:0, one launch (start us, length us, event | category | flops | bytes accessed | tf_op | source)
XLA Modules:
  0.0 139.0 jit_solution(9031705115320277429)
XLA Ops:
  0.0 137.5 %shard_map.73 = f32[128,256]{1,0:T(8,128)} custom-call(f32[32,65536]{1,0:T(8,128)} %sens_ref.1, s32[32]{0:T(128)} %period_ref.1, s32[32]{0:T(128)} %site_ref.1, f32[32]{0:T(128)} %period_err_ref.1, f32[128]{0:T(128)} %site_err_ref.1, s32[65536]{0:T(1024)} %perm_ref.1, f32[65536]{0:T(1024)} %var_ref.1), custom_call_target="tpu_custom_call" | custom-call | flops 4294967296 | bytes 8388608 | tf_op jit(solution)/shard_map/pallas_call | solution.py:318
  137.5 1.6 %copy.9 = f32[128,256]{1,0:T(8,128)} copy(f32[128,256]{1,0:T(8,128)} %shard_map.73) | data formatting | bytes 262144
